TPU v7x, 256 devices: a whole 4x4x8 slice. The times are simulated.
256 devices in a mesh: rep: 16 (over x_hi, z), fsdp: 16 (over x_lo, y, core).
Axes of the slice: x: 4 (x_hi: 2, x_lo: 2; x = x_hi * 2 + x_lo), y: 4, z: 8, core: 2. Of those that a mesh axis runs over, the one named last changes fastest.
Arguments:
- activations: bfloat16 [98304, 8192], P(('rep', 'fsdp')), may hold values from -6 to 6
- cotangent: bfloat16 [98304, 512], P(('rep', 'fsdp')), may hold values from -0.078125 to 0.078125
- momentum: float32 [16, 8192, 512], P('rep', 'fsdp'), may hold values from -6 to 6
- params: float32 [8192, 512], P('fsdp'), may hold values from -6 to 6
- band: int32 [128, 8, 32], P('fsdp'), may hold values from 0 to 975, as said below
Outputs:
- new_weights: bfloat16 [8192, 512], replicated
- new_momentum: float32 [16, 8192, 512], P('rep', 'fsdp')
Inputs may be any that keep to these rules, and one draw needn't show every extreme that they name: `band`: in every span the 32 positions are distinct, lie in rows 0 to 15 and columns 0 to 15 of the span's coefficients, and include 0 and 975.
All inputs are finite; a program needn't handle non-finite values.
Results may differ from a plain program's by a relative error of at most 0.001.
Values may be sent and summed in bfloat16 or wider, within the bound.
A program may use at most 128 MiB of HBM per device.

v0:
```python
import jax
import jax.numpy as jnp
from jax import lax
from jax.sharding import PartitionSpec as P

beta_decay = 0.9
step_size = 32.0


def dct_matrix():
    frequency = jnp.arange(64, dtype=jnp.float32)[:, None]
    position = jnp.arange(64, dtype=jnp.float32)[None, :]
    scaling = jnp.where(frequency == 0, jnp.sqrt(1.0 / 64.0), jnp.sqrt(2.0 / 64.0))
    return scaling * jnp.cos(jnp.pi * (2.0 * position + 1.0) * frequency / 128.0)


def forward_blocks(field, matrix):
    rows = field.shape[0]
    columns = field.shape[1]
    tiles = field.reshape(rows // 64, 64, columns // 64, 64)
    coefs = jnp.einsum("ki,aibj,lj->akbl", matrix, tiles, matrix, precision=lax.Precision.HIGHEST)
    return coefs.reshape(rows, columns)


def inverse_blocks(coefs, matrix):
    rows = coefs.shape[0]
    columns = coefs.shape[1]
    tiles = coefs.reshape(rows // 64, 64, columns // 64, 64)
    field = jnp.einsum("ki,akbl,lj->aibj", matrix, tiles, matrix, precision=lax.Precision.HIGHEST)
    return field.reshape(rows, columns)


def local(activations, cotangent, momentum, params, band):
    local_rows = params.shape[0]
    columns = params.shape[1]
    replicas = lax.axis_size("rep")
    contract = (((0,), (0,)), ((), ()))
    gradient = lax.psum_scatter(
        lax.dot_general(activations, cotangent, contract, preferred_element_type=jnp.float32),
        "fsdp",
        scatter_dimension=0,
        tiled=True,
    )
    blended = beta_decay * momentum[0] + gradient
    matrix = dct_matrix()
    coefs = forward_blocks(blended, matrix)
    row_index = jnp.arange(local_rows // 64, dtype=jnp.int32)[:, None, None] * 64 + band // 64
    col_index = jnp.arange(columns // 64, dtype=jnp.int32)[None, :, None] * 64 + band % 64
    chosen = coefs[row_index, col_index]

    def inverse_sparse(values):
        sparse = jnp.zeros((local_rows, columns), jnp.float32).at[row_index, col_index].add(values)
        return inverse_blocks(sparse, matrix)

    total = lax.psum(chosen, "rep")
    residual = blended - inverse_sparse(chosen)
    update = inverse_sparse(total / replicas)
    new_rows = (params - step_size * update).astype(jnp.bfloat16)
    new_weights = lax.all_gather(new_rows, "fsdp", axis=0, tiled=True)
    return (new_weights, residual[None])


def solution(mesh):
    return jax.shard_map(
        local,
        mesh=mesh,
        in_specs=(
            P(("rep", "fsdp"), None),
            P(("rep", "fsdp"), None),
            P("rep", "fsdp", None),
            P("fsdp", None),
            P("fsdp", None, None),
        ),
        out_specs=(P(), P("rep", "fsdp", None)),
        check_vma=False,
    )
```

profile of v0, /device:TPU:1, one launch (start us, length us, event | category | flops | bytes accessed | tf_op | source)
XLA Modules:
  0.0 313.1 jit_solution(14148486891314695270)
XLA Ops:
  8.2 11.1 %fusion.48 = f32[8192,512]{1,0:T(8,128)} fusion(bf16[384,8192]{1,0:T(8,128)(2,1)} %param.5, bf16[384,512]{1,0:T(8,128)(2,1)S(1)} %copy-done), kind=kOutput, calls=%fused_computation.73 | convolution fusion | flops 3221225472 | bytes 23461888 | tf_op jit(solution)/shard_map/dot_general | solution.py:39
  20.4 102.3 %reduce-scatter.2.cloned.1.call-done = f32[512,512]{1,0:T(8,128)} async-done(((f32[8192,512]{1,0:T(8,128)}), f32[512,512]{1,0:T(8,128)}) %reduce-scatter.2.cloned.1.call-update) | async-done | bytes 1048592 | tf_op jit(solution)/shard_map/reduce_scatter | solution.py:38
  122.7 1.4 bitcast_add_fusion
  124.5 2.3 fusion.4
  126.9 2.0 convolution_bitcast_fusion.1
  128.9 2.5 copy.8
  131.4 1.9 reshape.51
  133.3 16.6 %gather_fusion = f32[2048]{0:T(1024)S(1)} fusion(f32[512,512]{1,0:T(8,128)S(1)} %reshape.51, s32[2048]{0:T(1024)S(1)} %reshape.65), kind=kCustom, calls=%fused_computation | custom fusion | bytes 32768 | tf_op jit(solution)/shard_map/gather | solution.py:49
  150.0 63.5 %psum.7 = f32[8,8,32]{2,1,0:T(8,128)S(1)} all-reduce(f32[8,8,32]{2,1,0:T(8,128)S(1)} %reshape.68), channel_id=1, replica_groups=mesh['rep'=16,'fsdp'=16] {'rep'}, use_global_device_ids=true, to_apply=%region_1.2 | all-reduce | flops 2048 | bytes 16384 | tf_op jit(solution)/shard_map/psum | solution.py:55
  213.6 12.2 %scatter_custom_fusion = f32[262144]{0:T(1024)} fusion(s32[2048]{0:T(1024)S(1)} %reshape.71, f32[2048]{0:T(1024)S(1)} %reshape.73, f32[]{:T(128)} %constant.20.clone.1), kind=kCustom, calls=%fused_computation.17 | custom fusion | flops 2048 | bytes 1048580
  225.9 1.6 reshape.52
  227.5 2.3 fusion.2
  229.8 2.0 multiply_bitcast_fusion
  231.8 1.2 copy.9
  233.0 1.5 mul.166
  234.5 2.5 subtract_convert_fusion
  237.0 12.2 %scatter_custom_fusion.1 = f32[262144]{0:T(1024)} fusion(s32[2048]{0:T(1024)S(1)} %reshape.71, f32[2048]{0:T(1024)S(1)} %gather_fusion, f32[]{:T(128)} %constant.20.clone.1), kind=kCustom, calls=%fused_computation.15 | custom fusion | flops 2048 | bytes 1048580
  249.2 1.6 reshape.53
  250.8 2.3 fusion
  253.1 2.0 convolution_bitcast_fusion
  256.3 1.5 reshape.54
  257.8 2.4 subtract_bitcast_fusion
  260.2 38.7 %all-gather.2.cloned.1.call-done = bf16[8192,512]{1,0:T(8,128)(2,1)} async-done(((bf16[512,512]{1,0:T(8,128)(2,1)}), bf16[8192,512]{1,0:T(8,128)(2,1)}) %all-gather.2.cloned.1.call-update) | async-done | bytes 8388624 | tf_op jit(solution)/shard_map/all_gather | solution.py:59
  298.9 7.4 %copy.22 = bf16[8192,512]{1,0:T(8,128)(2,1)} copy(bf16[8192,512]{1,0:T(8,128)(2,1)} %all-gather.2.cloned.1.call-done) | data formatting | bytes 16777216
  (27 shorter events, 3.9 us)
Async XLA Ops:
  7.2 1.0 copy-start
  7.2 115.5 %reduce-scatter.2.cloned.1.call-start = ((), (), s32[]{:S(2)}) async-start(), calls=%async_computation.1 | async-start | bytes 17825792 | tf_op jit(solution)/shard_map/reduce_scatter | solution.py:38
  19.2 0.8 copy-start.3
  19.3 1.0 copy-start.4
  19.3 103.4 %copy-start.2 = (f32[1,512,512]{2,1,0:T(8,128)S(1)}, f32[1,512,512]{2,1,0:T(8,128)}, u32[]{:S(2)}) copy-start(f32[1,512,512]{2,1,0:T(8,128)} %param.7) | copy-start | bytes 3145732
  19.3 279.6 %all-gather.2.cloned.1.call-start = ((), (), s32[]{:S(2)}) async-start(), calls=%async_computation.2 | async-start | bytes 8912896 | tf_op jit(solution)/shard_map/all_gather | solution.py:59
  298.9 7.4 %copy-start.1 = (bf16[384,512]{1,0:T(8,128)(2,1)S(1)}, bf16[384,512]{1,0:T(8,128)(2,1)}, u32[]{:S(2)}) copy-start(bf16[384,512]{1,0:T(8,128)(2,1)} %param.6) | copy-start | bytes 1179652
Sparse Core Ops, SparseCore 0:
  19.4 103.2 reduce-scatter.1
  237.1 61.7 all-gather.1
where the time goes:
time: 314 us; the launch traced here: 313 us
  waiting for transfers between devices  141 us (45%)
  blocking collectives  63.5 us (20%)
  local copies, waits for them, and re-layouts  39.3 us (13%)
  other arithmetic  31 us (10%)
  matrix products  24 us (8%)
  between operations  14.2 us (5%)
    reduce_scatter x1, waiting for transfers between devices, local(): lax.psum_scatter(lax.dot_general(activations, cotangent, contract, prefer...  102 us
    psum x1, blocking collectives, local(): total = lax.psum(chosen, 'rep')  63.5 us
    all_gather x1, waiting for transfers between devices, local(): new_weights = lax.all_gather(new_rows, 'fsdp', axis=0, tiled=True)  38.7 us
    unnamed x5, other arithmetic  24.6 us
    gather x2, local copies, waits for them, and re-layouts, local(): chosen = coefs[row_index, col_index]  16.7 us
    dot_general x1, matrix products, local(): lax.dot_general(activations, cotangent, contract, preferred_element_type=...  11.1 us
    unnamed x12, local copies, waits for them, and re-layouts  9.07 us
    dot_general x4, matrix products, inverse_blocks(): jnp.einsum('ki,akbl,lj->aibj', matrix, tiles, matrix, precision=lax.Preci...  8.63 us
  transfers between devices with their start and end apart: 2, of which 2 were waited for; matrix products, arithmetic and copies ran while one was open for 8% of the time, Pallas kernels for 0%

commit v1 on v0

v1 whole, which is shorter than its diff:
```python
import jax
import jax.numpy as jnp
import numpy as np
from jax import lax
from jax.experimental import pallas as pl
from jax.experimental.pallas import tpu as pltpu
from jax.sharding import PartitionSpec as P

MESH = pl.DeviceIdType.MESH
HIGHEST = lax.Precision.HIGHEST
beta_decay = 0.9
step_size = 32.0
N_REP = 16
ROWS = 512
COLS = 512
TOK = 384
QUARTER = 128
PACKED = 4 * QUARTER + 16
CODE = 64.0
FULL = 32000.0
X_LO_ROWS = 128

ORDER = [(1, 2), (0, 2), (1, 1), (1, 3), (0, 1), (0, 3), (1, 0), (0, 0)]


def band_matrix():
    frequency = np.arange(16)[:, None]
    position = np.arange(64)[None, :]
    scaling = np.where(frequency == 0, np.sqrt(1.0 / 64.0), np.sqrt(2.0 / 64.0))
    table = scaling * np.cos(np.pi * (2.0 * position + 1.0) * frequency / 128.0)
    return np.kron(np.eye(8), table).astype(np.float32)


def dot_last(a, b, precision=HIGHEST):
    return lax.dot_general(
        a, b, (((1,), (1,)), ((), ())), precision=precision, preferred_element_type=jnp.float32
    )


def dot(a, b, precision=HIGHEST):
    return lax.dot_general(
        a, b, (((1,), (0,)), ((), ())), precision=precision, preferred_element_type=jnp.float32
    )


def halves(x):
    high = x.astype(jnp.bfloat16)
    return high, (x - high.astype(jnp.float32)).astype(jnp.bfloat16)


MESSAGES = (
    [("x1", dy, q) for dy in (2, 1, 3, 0) for q in (0, 1)]
    + [(ring, part) for ring in ("b1", "b0", "a0") for part in ("p1lo", "p1hi", "p2hi", "p2lo", "p3lo", "p3hi")]
    + [("x3", q) for q in (2, 3)]
)
SLOT = {key: i for i, key in enumerate(MESSAGES)}
GATHERS = (
    [("core", dx, dy, part) for dx in (0, 1) for dy in range(4) for part in (0, 1)]
    + [("y+",), ("y-",), ("y++",), ("y--",)]
    + [("xlo", dy) for dy in range(4)]
    + [("xhi", dy) for dy in range(4)]
)
GATHER = {key: i for i, key in enumerate(GATHERS)}


def kernel(
    act_hbm, cot_hbm, mom_hbm, par_hbm, band_hbm, f_hbm, ft_hbm,
    new_w, new_m,
    act, cot, mom, par, band, fm, ftm, weights, g, head, base, mask, out_q, in_q,
    corner_out, corner_in, csum, slice_in, mean,
    local_sem, act_sem, act_send, act_recv, cot_send, cot_recv, q_send, q_recv, c_send, c_recv,
    r_send, r_recv, m_send, m_recv, w_send, w_recv,
):
    rep, fsdp = lax.axis_index("rep"), lax.axis_index("fsdp")
    x_hi, z = rep // 8, lax.rem(rep, 8)
    x_lo, y, core = fsdp // 8, lax.rem(fsdp // 2, 4), lax.rem(fsdp, 2)

    def chunk(dx, dy):
        return lax.rem(x_lo + dx, 2) * 4 + lax.rem(y + dy, 4)

    def shard(dx, dy, dc=0):
        return chunk(dx, dy) * 2 + lax.rem(core + dc, 2)

    def peer(dx, dy, dc=0):
        return (rep, shard(dx, dy, dc))

    def rep_peer(k):
        return (lax.rem(rep + k, N_REP), fsdp)

    x_hi_peer = (lax.rem(x_hi + 1, 2) * 8 + z, shard(1, 0))
    x_peer, up, down, sibling = peer(1, 0), peer(0, 1), peer(0, 3), peer(0, 0, 1)

    mine = [pltpu.make_async_copy(cot_hbm, cot.at[pl.ds(0, TOK)], local_sem.at[0])]
    mine[0].start()

    def act_local(dx, dy):
        i = chunk(dx, dy)
        column = pl.multiple_of((i * 2 + core) * ROWS, ROWS)
        return pltpu.make_async_copy(
            act_hbm.at[:, pl.ds(column, ROWS)], act.at[i, pl.ds(0, TOK)], act_sem.at[i]
        )

    for dx, dy in ORDER:
        act_local(dx, dy).start()
    for i, (src, dst) in enumerate(
        [(mom_hbm.at[0], mom), (par_hbm, par), (band_hbm, band), (f_hbm, fm), (ft_hbm, ftm)]
    ):
        mine.append(pltpu.make_async_copy(src, dst, local_sem.at[i + 1]))
        mine[-1].start()

    barrier = pltpu.get_barrier_semaphore()
    greeted = [sibling, x_hi_peer]
    greeted += [peer(dx, dy) for dx, dy in ORDER if (dx, dy) != (0, 0)]
    greeted += [rep_peer(k) for k in range(1, N_REP)]
    for other in greeted:
        pl.semaphore_signal(barrier, inc=1, device_id=other, device_id_type=MESH)
    pl.semaphore_wait(barrier, len(greeted))

    cot_copy = pltpu.make_async_remote_copy(
        src_ref=cot_hbm, dst_ref=cot.at[pl.ds(TOK, TOK)], send_sem=cot_send, recv_sem=cot_recv,
        device_id=sibling, device_id_type=MESH,
    )
    cot_copy.start()

    def act_copy(dx, dy):
        i = chunk(dx, dy)
        column = pl.multiple_of((i * 2 + 1 - core) * ROWS, ROWS)
        return pltpu.make_async_remote_copy(
            src_ref=act_hbm.at[:, pl.ds(column, ROWS)], dst_ref=act.at[i, pl.ds(TOK, TOK)],
            send_sem=act_send.at[i], recv_sem=act_recv.at[i], device_id=sibling, device_id_type=MESH,
        )

    for dx, dy in ORDER:
        act_copy(dx, dy).start()

    for copy in mine:
        copy.wait()
    cot_copy.wait()
    turned = cot[...].astype(jnp.float32).T.astype(jnp.bfloat16)
    weights[pl.ds(0, COLS), :] = turned
    f_high, f_low = halves(fm[...])
    low = dot(f_high, turned, None) + dot(f_low, turned, None)
    low_high, low_low = halves(low)
    weights[pl.ds(COLS, 128), :] = low_high
    weights[pl.ds(COLS + 128, 128), :] = low_low

    def rows_of(q, r, p):
        return pl.ds(pl.multiple_of(q * QUARTER + r * 32, 32), 32), pl.ds(p * 128, 128)

    def peak_of(i, q):
        def body(r, peak):
            for p in range(4):
                rows, lanes = rows_of(q, r, p)
                v = jnp.abs(g[i, rows, lanes])
                peak = jnp.maximum(peak, jnp.max(v.reshape(4, 8, 128), axis=0))
            return peak

        return lax.fori_loop(0, QUARTER // 32, body, jnp.zeros((8, 128), jnp.float32))

    def unpack(key, r, p):
        slot = SLOT[key]
        rows = pl.ds(pl.multiple_of(p * QUARTER + r * 32, 32), 32)
        return in_q[slot, rows, :].astype(jnp.int32).astype(jnp.float32)

    def scale_of(code):
        return jnp.exp(code.astype(jnp.int32).astype(jnp.float32) * (1.0 / CODE)) * (1.0 / FULL)

    def received_scale(key):
        code = in_q[SLOT[key], pl.ds(4 * QUARTER, 16), :]
        return scale_of(code)[0:1]

    def add_received(i, q, keys):
        scales = [received_scale(key) for key in keys]

        def body(r, peak):
            for p in range(4):
                rows, lanes = rows_of(q, r, p)
                v = g[i, rows, lanes]
                for key, scale in zip(keys, scales, strict=True):
                    v = v + unpack(key, r, p) * scale
                g[i, rows, lanes] = v
                peak = jnp.maximum(peak, jnp.max(jnp.abs(v).reshape(4, 8, 128), axis=0))
            return peak

        return lax.fori_loop(0, QUARTER // 32, body, jnp.zeros((8, 128), jnp.float32))

    def message(key, target):
        slot = SLOT[key]
        return pltpu.make_async_remote_copy(
            src_ref=out_q.at[slot], dst_ref=in_q.at[slot], send_sem=q_send.at[slot],
            recv_sem=q_recv.at[slot], device_id=target, device_id_type=MESH,
        )

    target_of = {"p1lo": up, "p1hi": down, "p2hi": up, "p2lo": down, "p3lo": up, "p3hi": down}

    def message_of(key):
        return message(key, x_peer if key[0] in ("x1", "x3") else target_of[key[1]])

    def send(key, i, q, peak):
        slot = SLOT[key]
        peak = jnp.max(peak, axis=0, keepdims=True)
        code = jnp.ceil(jnp.log(jnp.maximum(peak, 1e-30)) * CODE) + 1.0
        code = jnp.broadcast_to(code, (16, 128)).astype(jnp.int32).astype(jnp.int16)
        out_q[slot, pl.ds(4 * QUARTER, 16), :] = code
        inverse = 1.0 / scale_of(code)[0:1]

        def body(r, carry):
            for p in range(4):
                rows, lanes = rows_of(q, r, p)
                v = jnp.round(g[i, rows, lanes] * inverse).astype(jnp.int32).astype(jnp.int16)
                out_q[slot, pl.ds(pl.multiple_of(p * QUARTER + r * 32, 32), 32), :] = v
            return carry

        lax.fori_loop(0, QUARTER // 32, body, 0)
        message_of(key).start()

    def arrived(*keys):
        for key in keys:
            message_of(key).wait_recv()

    def corner_copy(dx, dy):
        k = dx * 4 + dy
        return pltpu.make_async_remote_copy(
            src_ref=corner_out.at[k], dst_ref=corner_in.at[k], send_sem=c_send.at[k],
            recv_sem=c_recv.at[k], device_id=peer(dx, dy), device_id_type=MESH,
        )

    for dx, dy in ORDER:
        i = chunk(dx, dy)
        act_local(dx, dy).wait()
        act_copy(dx, dy).wait()

        def product(n, carry, i=i):
            lanes = pl.ds(pl.multiple_of(n * 256, 256), 256)
            both = dot(weights[...], act[i, :, lanes], None)
            g[i, :, lanes] = both[:COLS]
            head[:, lanes] = both[COLS : COLS + 128] + both[COLS + 128 :]
            return carry

        lax.fori_loop(0, ROWS // 256, product, 0)
        corner_out[dx * 4 + dy] = dot_last(head[...], fm[...])
        if (dx, dy) != (0, 0):
            corner_copy(dx, dy).start()
        sends = []
        if dx == 1:
            sends += [(("x1", dy, q), q) for q in (0, 1)]
        ring = "b1" if dx else "b0"
        sends += {2: [((ring, "p1lo"), 2), ((ring, "p1hi"), 3)], 1: [((ring, "p2hi"), 3)], 3: [((ring, "p2lo"), 2)], 0: []}[dy]
        for key, q in sends:
            send(key, i, q, peak_of(i, q))

    lane = lax.broadcasted_iota(jnp.int32, (8, 128), 1)
    pick = jnp.where(lane // 16 == lax.broadcasted_iota(jnp.int32, (8, 128), 0), 1.0, 0.0)
    offset = (lax.rem(lax.broadcasted_iota(jnp.int32, (32, 128), 1), 16) * 64).astype(jnp.float32)
    column = lax.broadcasted_iota(jnp.int32, (16, 32, 128), 0).astype(jnp.float32)
    for b in range(8):
        places = band[:, b, :].astype(jnp.float32)
        spread = lax.dot_general(
            places, pick, (((0,), (0,)), ((), ())), precision=HIGHEST, preferred_element_type=jnp.float32
        )
        hit = jnp.where((spread - offset)[None] == column, 1.0, 0.0)
        mask[pl.ds(b * 16, 16), :] = jnp.max(hit, axis=1)
    momentum_low = dot_last(dot_last(fm[...], mom[...]), fm[...]) * beta_decay

    for ring, dx in (("b1", 1), ("b0", 0)):
        arrived((ring, "p1lo"))
        send((ring, "p3lo"), chunk(dx, 1), 2, add_received(chunk(dx, 1), 2, [(ring, "p1lo")]))
        arrived((ring, "p1hi"))
        send((ring, "p3hi"), chunk(dx, 3), 3, add_received(chunk(dx, 3), 3, [(ring, "p1hi")]))

    total = corner_out[0] + momentum_low
    for dx, dy in ORDER[:-1]:
        corner_copy(dx, dy).wait()
        total = total + corner_in[dx * 4 + dy]
    csum[...] = total

    def slice_rows(k):
        return pl.ds(pl.multiple_of(lax.rem(rep + k, N_REP) * 8, 8), 8)

    def slice_copy(k):
        return pltpu.make_async_remote_copy(
            src_ref=csum.at[slice_rows(k)], dst_ref=slice_in.at[k], send_sem=r_send.at[k],
            recv_sem=r_recv.at[k], device_id=rep_peer(k), device_id_type=MESH,
        )

    for k in range(1, N_REP):
        slice_copy(k).start()

    arrived(("x1", 2, 0))
    send(("a0", "p1lo"), chunk(0, 2), 0, add_received(chunk(0, 2), 0, [("x1", 2, 0)]))
    arrived(("x1", 2, 1))
    send(("a0", "p1hi"), chunk(0, 2), 1, add_received(chunk(0, 2), 1, [("x1", 2, 1)]))

    for k in range(1, N_REP):
        slice_copy(k).wait()
    part = csum[slice_rows(0), :]
    for k in range(1, N_REP):
        part = part + slice_in[k]
    mean[slice_rows(0), :] = part * (1.0 / N_REP)

    def mean_copy(k):
        return pltpu.make_async_remote_copy(
            src_ref=mean.at[slice_rows(0)], dst_ref=mean.at[slice_rows(0)], send_sem=m_send.at[k],
            recv_sem=m_recv.at[k], device_id=rep_peer(k), device_id_type=MESH,
        )

    for k in range(1, N_REP):
        mean_copy(k).start()

    arrived(("x1", 1, 1))
    send(("a0", "p2hi"), chunk(0, 1), 1, add_received(chunk(0, 1), 1, [("x1", 1, 1)]))
    arrived(("x1", 3, 0))
    send(("a0", "p2lo"), chunk(0, 3), 0, add_received(chunk(0, 3), 0, [("x1", 3, 0)]))

    def inverse(coefs):
        return dot(dot_last(ftm[...], coefs * mask[...]), fm[...])

    base[...] = beta_decay * mom[...] - inverse(csum[...])

    for k in range(1, N_REP):
        mean_copy(k).wait()

    def chunk_rows(dx, dy, dc=0, first=0, count=ROWS):
        return pl.ds(pl.multiple_of(shard(dx, dy, dc) * ROWS + first, 16), count)

    new_w[chunk_rows(0, 0), :] = (par[...] - step_size * inverse(mean[...])).astype(jnp.bfloat16)

    def gather_copy(key, rows, target):
        k = GATHER[key]
        return pltpu.make_async_remote_copy(
            src_ref=new_w.at[rows], dst_ref=new_w.at[rows], send_sem=w_send.at[k],
            recv_sem=w_recv.at[k], device_id=target, device_id_type=MESH,
        )

    copies = {}

    def gather(key, rows, target):
        copies[key] = gather_copy(key, rows, target)
        copies[key].start()

    gather(("y+",), chunk_rows(0, 0), up)
    gather(("y-",), chunk_rows(0, 0), down)

    def share(dy):
        gather(("xlo", dy), chunk_rows(0, dy, 0, 0, X_LO_ROWS), x_peer)
        gather(("xhi", dy), chunk_rows(0, dy, 0, X_LO_ROWS, ROWS - X_LO_ROWS), x_hi_peer)

    share(0)
    gather(("core", 0, 0, 0), chunk_rows(0, 0), sibling)

    arrived(("b1", "p2lo"), ("b1", "p3lo"))
    send(("x3", 2), chunk(1, 0), 2, add_received(chunk(1, 0), 2, [("b1", "p2lo"), ("b1", "p3lo")]))
    arrived(("b1", "p2hi"), ("b1", "p3hi"))
    send(("x3", 3), chunk(1, 0), 3, add_received(chunk(1, 0), 3, [("b1", "p2hi"), ("b1", "p3hi")]))

    arrived(("x1", 1, 0), ("a0", "p1lo"))
    send(("a0", "p3lo"), chunk(0, 1), 0, add_received(chunk(0, 1), 0, [("x1", 1, 0), ("a0", "p1lo")]))
    arrived(("x1", 3, 1), ("a0", "p1hi"))
    send(("a0", "p3hi"), chunk(0, 3), 1, add_received(chunk(0, 3), 1, [("x1", 3, 1), ("a0", "p1hi")]))

    copies[("y+",)].wait_recv()
    gather(("y++",), chunk_rows(0, 3, 0, 0, ROWS // 2), up)
    share(3)
    gather(("core", 0, 3, 0), chunk_rows(0, 3), sibling)
    copies[("y-",)].wait_recv()
    gather(("y--",), chunk_rows(0, 1, 0, ROWS // 2, ROWS // 2), down)
    share(1)
    gather(("core", 0, 1, 0), chunk_rows(0, 1), sibling)

    def finish(q, keys):
        arrived(*keys)
        add_received(chunk(0, 0), q, keys)
        lanes = pl.ds(q * QUARTER, QUARTER)
        new_m[0, :, lanes] = base[:, lanes] + g[chunk(0, 0), lanes, :].T

    finish(2, [("b0", "p2lo"), ("b0", "p3lo"), ("x3", 2)])
    finish(3, [("b0", "p2hi"), ("b0", "p3hi"), ("x3", 3)])

    copies[("y++",)].wait_recv()
    copies[("y--",)].wait_recv()
    share(2)
    gather(("core", 0, 2, 0), chunk_rows(0, 2), sibling)
    finish(0, [("x1", 0, 0), ("a0", "p2lo"), ("a0", "p3lo")])
    finish(1, [("x1", 0, 1), ("a0", "p2hi"), ("a0", "p3hi")])

    for dy in (0, 3, 1, 2):
        copies[("xlo", dy)].wait_recv()
        gather(("core", 1, dy, 0), chunk_rows(1, dy, 0, 0, X_LO_ROWS), sibling)
        copies[("xhi", dy)].wait_recv()
        gather(("core", 1, dy, 1), chunk_rows(1, dy, 0, X_LO_ROWS, ROWS - X_LO_ROWS), sibling)

    for key, copy in copies.items():
        copy.wait_send()
        if key[0] == "core":
            copy.wait_recv()
    for key in MESSAGES:
        message_of(key).wait_send()


def local(activations, cotangent, momentum, params, band, f, ft):
    any_space = pl.BlockSpec(memory_space=pl.ANY)
    i16, f32, bf16 = jnp.int16, jnp.float32, jnp.bfloat16
    dma = pltpu.SemaphoreType.DMA
    n = len(MESSAGES)
    return pl.pallas_call(
        kernel,
        out_shape=(
            pltpu.VMEM((16 * ROWS, COLS), bf16),
            pltpu.VMEM((1, ROWS, COLS), f32),
        ),
        in_specs=[any_space] * 7,
        out_specs=(pl.BlockSpec(memory_space=pltpu.VMEM), pl.BlockSpec(memory_space=pltpu.VMEM)),
        scratch_shapes=[
            pltpu.VMEM((8, 2 * TOK, ROWS), bf16),
            pltpu.VMEM((2 * TOK, COLS), bf16),
            pltpu.VMEM((ROWS, COLS), f32),
            pltpu.VMEM((ROWS, COLS), f32),
            pltpu.VMEM((8, 8, 32), jnp.int32),
            pltpu.VMEM((128, 512), f32),
            pltpu.VMEM((512, 128), f32),
            pltpu.VMEM((COLS + 256, 2 * TOK), bf16),
            pltpu.VMEM((8, COLS, ROWS), f32),
            pltpu.VMEM((128, ROWS), f32),
            pltpu.VMEM((ROWS, COLS), f32),
            pltpu.VMEM((128, 128), f32),
            pltpu.VMEM((n, PACKED, 128), i16),
            pltpu.VMEM((n, PACKED, 128), i16),
            pltpu.VMEM((8, 128, 128), f32),
            pltpu.VMEM((8, 128, 128), f32),
            pltpu.VMEM((128, 128), f32),
            pltpu.VMEM((N_REP, 8, 128), f32),
            pltpu.VMEM((128, 128), f32),
            dma((6,)), dma((8,)), dma((8,)), dma((8,)), dma, dma, dma((n,)), dma((n,)), dma((8,)), dma((8,)),
            dma((N_REP,)), dma((N_REP,)), dma((N_REP,)), dma((N_REP,)), dma((len(GATHERS),)), dma((len(GATHERS),)),
        ],
        compiler_params=pltpu.CompilerParams(
            collective_id=0, has_side_effects=True, vmem_limit_bytes=48 * 2**20
        ),
    )(activations, cotangent, momentum, params, band, f, ft)


def step(activations, cotangent, momentum, params, band):
    f = band_matrix()
    return local(activations, cotangent, momentum, params, band, jnp.asarray(f), jnp.asarray(f.T.copy()))


def solution(mesh):
    return jax.shard_map(
        step,
        mesh=mesh,
        in_specs=(
            P(("rep", "fsdp"), None),
            P(("rep", "fsdp"), None),
            P("rep", "fsdp", None),
            P("fsdp", None),
            P("fsdp", None, None),
        ),
        out_specs=(P(), P("rep", "fsdp", None)),
        check_vma=False,
    )
```

time: 314 us -> 101 us (0.32)
  waiting for transfers between devices: 141 us -> 0 us
  Pallas kernels: 0 us -> 96.2 us
  blocking collectives: 63.5 us -> 0 us
  local copies, waits for them, and re-layouts: 39.3 us -> 4.37 us
  other arithmetic: 31 us -> 0 us
  matrix products: 24 us -> 0 us
  between operations: 14.2 us -> 0.64 us
    reduce_scatter x1 -> x0, waiting for transfers between devices: 102 us -> none  [local(): lax.psum_scatter(lax.dot_general(activations, cotangent, contract, prefer...]
    pallas_call x0 -> x1, Pallas kernels: none -> 96.2 us  [local(): pl.pallas_call(kernel, out_shape=(pltpu.VMEM((16 * ROWS, COLS), bf16), pl...]
    psum x1 -> x0, blocking collectives: 63.5 us -> none  [local(): total = lax.psum(chosen, 'rep')]
    all_gather x1 -> x0, waiting for transfers between devices: 38.7 us -> none  [local(): new_weights = lax.all_gather(new_rows, 'fsdp', axis=0, tiled=True)]
    unnamed x5 -> x0, other arithmetic: 24.6 us -> none
    dot_general x7 -> x0, matrix products: 24 us -> none  [the longest x1 11.1 us: local(): lax.dot_general(activations, cotangent, contract, preferred_element_type=...]
    gather x2 -> x0, local copies, waits for them, and re-layouts: 16.7 us -> none  [local(): chosen = coefs[row_index, col_index]]
    reshape x5 -> x0, local copies, waits for them, and re-layouts: 6.96 us -> none  [the longest x2 3.15 us: inverse_blocks(): tiles = coefs.reshape(rows // 64, 64, columns // 64, 64)]
  transfers between devices with their start and end apart: 2 -> 0, of which waited for: 2 -> 0; matrix products, arithmetic and copies ran while one was open for 8% -> 0% of each run, Pallas kernels for 0% -> 0%
where the time goes in v1:
time: 101 us
  Pallas kernels  96.2 us (95%)
  local copies, waits for them, and re-layouts  4.37 us (4%)
    pallas_call x1, Pallas kernels, local(): pl.pallas_call(kernel, out_shape=(pltpu.VMEM((16 * ROWS, COLS), bf16), pl...  96.2 us
    unnamed x2, local copies, waits for them, and re-layouts  4.37 us

profile of v1, /device:TPU:1, one launch (start us, length us, event | category | flops | bytes accessed | tf_op | source)
XLA Modules:
  0.0 101.3 jit_solution(10110695727495542888)
XLA Ops:
  0.6 96.2 %shard_map.86 = (bf16[8192,512]{1,0:T(8,128)(2,1)S(1)}, f32[1,512,512]{2,1,0:T(8,128)S(1)}) custom-call(bf16[384,8192]{1,0:T(8,128)(2,1)} %act_hbm.1, bf16[384,512]{1,0:T(8,128)(2,1)} %cot_hbm.1, f32[1,512,512]{2,1,0:T(8,128)} %mom_hbm.1, f32[512,512]{1,0:T(8,128)} %par_hbm.1, s32[8,8,32]{2,1,0:T(8,128)} %band_hbm.1, f32[128,512]{1,0:T(8,128)} %constant.4.clone.f_hbm, ...), custom_call_target="tpu_custom_call" | custom-call | tf_op jit(solution)/shard_map/pallas_call | solution.py:405
  96.9 3.4 %copy.11 = bf16[8192,512]{1,0:T(8,128)(2,1)} copy(bf16[8192,512]{1,0:T(8,128)(2,1)S(1)} %get-tuple-element.2) | data formatting | bytes 16777216
  100.3 1.0 copy.12

commit v2 on v1

v2 whole, which is shorter than its diff:
```python
import jax
import jax.numpy as jnp
import numpy as np
from jax import lax
from jax.experimental import pallas as pl
from jax.experimental.pallas import tpu as pltpu
from jax.sharding import PartitionSpec as P

MESH = pl.DeviceIdType.MESH
HIGHEST = lax.Precision.HIGHEST
beta_decay = 0.9
step_size = 32.0
N_REP = 16
ROWS = 512
COLS = 512
TOK = 384
QUARTER = 128
PACKED = 4 * QUARTER + 16
CODE = 64.0
FULL = 32000.0
KEPT = 64
PART = (ROWS - KEPT) // 4

ORDER = [(1, 2), (0, 2), (1, 1), (1, 3), (0, 1), (0, 3), (1, 0), (0, 0)]


def band_matrix():
    frequency = np.arange(16)[:, None]
    position = np.arange(64)[None, :]
    scaling = np.where(frequency == 0, np.sqrt(1.0 / 64.0), np.sqrt(2.0 / 64.0))
    table = scaling * np.cos(np.pi * (2.0 * position + 1.0) * frequency / 128.0)
    return np.kron(np.eye(8), table).astype(np.float32)


def dot_last(a, b, precision=HIGHEST):
    return lax.dot_general(
        a, b, (((1,), (1,)), ((), ())), precision=precision, preferred_element_type=jnp.float32
    )


def dot(a, b, precision=HIGHEST):
    return lax.dot_general(
        a, b, (((1,), (0,)), ((), ())), precision=precision, preferred_element_type=jnp.float32
    )


def halves(x):
    high = x.astype(jnp.bfloat16)
    return high, (x - high.astype(jnp.float32)).astype(jnp.bfloat16)


MESSAGES = (
    [("x1", dy, q) for dy in (2, 1, 3, 0) for q in (0, 1)]
    + [(ring, part) for ring in ("b1", "b0", "a0") for part in ("p1lo", "p1hi", "p2hi", "p2lo", "p3lo", "p3hi")]
    + [("x3", q) for q in (2, 3)]
)
SLOT = {key: i for i, key in enumerate(MESSAGES)}
OTHERS = [(dx, dy) for dx in (0, 1) for dy in range(4) if (dx, dy) != (0, 0)]
GATHERS = (
    [("core", dx, dy, p) for dx in (0, 1) for dy in range(4) for p in (0, 1, 2)]
    + [("corez", dx, dy) for dx, dy in OTHERS]
    + [(way, p) for way in ("y+", "y-") for p in (0, 1, 2)]
    + [(way, p) for way in ("y++", "y--") for p in (0, 1)]
    + [("x", dy, p) for dy in range(4) for p in (0, 1, 2)]
    + [(way, dx, dy) for way in ("z+", "z-") for dx, dy in OTHERS]
)
GATHER = {key: i for i, key in enumerate(GATHERS)}


def kernel(
    act_hbm, cot_hbm, mom_hbm, par_hbm, band_hbm, f_hbm, ft_hbm,
    new_w, new_m,
    act, act2, cot, mom, par, band, fm, ftm, low_parts, ft_parts, weights, g, base, column, here, out_q, in_q,
    corners, corners2, corner_out, corner_in, sent, sent_in, spread_values, coefs, low_sum,
    local_sem, act_sem, act_send, act_recv, sib_send, sib_recv, q_send, q_recv, c_send, c_recv,
    r_send, r_recv, w_send, w_recv,
):
    rep, fsdp = lax.axis_index("rep"), lax.axis_index("fsdp")
    x_hi, z = rep // 8, lax.rem(rep, 8)
    x_lo, y, core = fsdp // 8, lax.rem(fsdp // 2, 4), lax.rem(fsdp, 2)

    def chunk(dx, dy):
        return lax.rem(x_lo + dx, 2) * 4 + lax.rem(y + dy, 4)

    def shard(dx, dy, dc=0):
        return chunk(dx, dy) * 2 + lax.rem(core + dc, 2)

    def peer(dx, dy, dc=0):
        return (rep, shard(dx, dy, dc))

    def rep_peer(k):
        return (lax.rem(rep + k, N_REP), fsdp)

    x_hi_peer = (lax.rem(x_hi + 1, 2) * 8 + z, shard(1, 0))
    x_peer, up, down, sibling = peer(1, 0), peer(0, 1), peer(0, 3), peer(0, 0, 1)
    ahead = (x_hi * 8 + lax.rem(z + 1, 8), fsdp)
    behind = (x_hi * 8 + lax.rem(z + 7, 8), fsdp)

    barrier = pltpu.get_barrier_semaphore()
    greeted = [rep_peer(k) for k in range(1, N_REP)] + [x_hi_peer, sibling]
    greeted += [peer(dx, dy) for dx, dy in ORDER[:-1]]
    for other in greeted:
        pl.semaphore_signal(barrier, inc=1, device_id=other, device_id_type=MESH)

    def load(src, dst, i):
        copy = pltpu.make_async_copy(src, dst, local_sem.at[i])
        copy.start()
        return copy

    first = [load(cot_hbm, cot, 0), load(f_hbm, fm, 1), load(ft_hbm, ftm, 4)]

    def act_local(i):
        lanes = pl.ds(pl.multiple_of(i * 2 * ROWS, 2 * ROWS), 2 * ROWS)
        return pltpu.make_async_copy(act_hbm.at[:, lanes], act.at[:, lanes], act_sem.at[i])

    for i in range(8):
        act_local(i).start()
    second = [load(band_hbm, band, 2), load(mom_hbm.at[0], mom, 3), load(par_hbm, par, 5)]

    for copy in first:
        copy.wait()
    turned = cot[...].astype(jnp.float32).T.astype(jnp.bfloat16)
    weights[:, pl.ds(0, TOK)] = turned
    low = dot(jnp.concatenate(halves(fm[...]), axis=0), turned, None)
    low_parts[...] = jnp.concatenate(halves(low[:128] + low[128:]), axis=0)
    ft_parts[...] = jnp.concatenate(halves(ftm[...]), axis=1)

    def corner(i, carry):
        act_local(i).wait()
        for half in (0, 1):
            lanes = pl.ds(pl.multiple_of((i * 2 + half) * ROWS, ROWS), ROWS)
            both = dot(low_parts[...], act[:, lanes], None)
            both = jnp.concatenate(halves(both[:128] + both[128:]), axis=0)
            both = dot(both, ft_parts[...], None)
            corners[half, i] = both[:128, :128] + (both[:128, 128:] + both[128:, :128])
        return carry

    lax.fori_loop(0, 8, corner, 0)

    pl.semaphore_wait(barrier, len(greeted))

    def to_sibling(src, dst, i):
        return pltpu.make_async_remote_copy(
            src_ref=src, dst_ref=dst, send_sem=sib_send.at[i], recv_sem=sib_recv.at[i],
            device_id=sibling, device_id_type=MESH,
        )

    corner_swap = to_sibling(corners.at[1 - core], corners2, 0)
    corner_swap.start()
    weight_swap = to_sibling(weights.at[:, pl.ds(0, TOK)], weights.at[:, pl.ds(TOK, TOK)], 1)
    weight_swap.start()

    def act_copy(dx, dy):
        i = chunk(dx, dy)
        lanes = pl.ds(pl.multiple_of((i * 2 + 1 - core) * ROWS, ROWS), ROWS)
        return pltpu.make_async_remote_copy(
            src_ref=act.at[:, lanes], dst_ref=act2.at[i],
            send_sem=act_send.at[i], recv_sem=act_recv.at[i], device_id=sibling, device_id_type=MESH,
        )

    for dx, dy in ORDER:
        act_copy(dx, dy).start()

    def rows_of(q, r, p):
        return pl.ds(pl.multiple_of(q * QUARTER + r * 32, 32), 32), pl.ds(p * 128, 128)

    def peak_of(i, q):
        def body(r, peak):
            for p in range(4):
                rows, lanes = rows_of(q, r, p)
                v = jnp.abs(g[i, rows, lanes])
                peak = jnp.maximum(peak, jnp.max(v.reshape(4, 8, 128), axis=0))
            return peak

        return lax.fori_loop(0, QUARTER // 32, body, jnp.zeros((8, 128), jnp.float32))

    def unpack(key, r, p):
        slot = SLOT[key]
        rows = pl.ds(pl.multiple_of(p * QUARTER + r * 32, 32), 32)
        return in_q[slot, rows, :].astype(jnp.int32).astype(jnp.float32)

    def scale_of(code):
        return jnp.exp(code.astype(jnp.int32).astype(jnp.float32) * (1.0 / CODE)) * (1.0 / FULL)

    def received_scale(key):
        code = in_q[SLOT[key], pl.ds(4 * QUARTER, 16), :]
        return scale_of(code)[0:1]

    def add_received(i, q, keys):
        scales = [received_scale(key) for key in keys]

        def body(r, peak):
            for p in range(4):
                rows, lanes = rows_of(q, r, p)
                v = g[i, rows, lanes]
                for key, scale in zip(keys, scales, strict=True):
                    v = v + unpack(key, r, p) * scale
                g[i, rows, lanes] = v
                peak = jnp.maximum(peak, jnp.max(jnp.abs(v).reshape(4, 8, 128), axis=0))
            return peak

        return lax.fori_loop(0, QUARTER // 32, body, jnp.zeros((8, 128), jnp.float32))

    def message(key, target):
        slot = SLOT[key]
        return pltpu.make_async_remote_copy(
            src_ref=out_q.at[slot], dst_ref=in_q.at[slot], send_sem=q_send.at[slot],
            recv_sem=q_recv.at[slot], device_id=target, device_id_type=MESH,
        )

    target_of = {"p1lo": up, "p1hi": down, "p2hi": up, "p2lo": down, "p3lo": up, "p3hi": down}

    def message_of(key):
        return message(key, x_peer if key[0] in ("x1", "x3") else target_of[key[1]])

    def send(key, i, q, peak):
        slot = SLOT[key]
        peak = jnp.max(peak, axis=0, keepdims=True)
        code = jnp.broadcast_to(code_of(peak), (16, 128)).astype(jnp.int32).astype(jnp.int16)
        out_q[slot, pl.ds(4 * QUARTER, 16), :] = code
        inverse = 1.0 / scale_of(code)[0:1]

        def body(r, carry):
            for p in range(4):
                rows, lanes = rows_of(q, r, p)
                v = jnp.round(g[i, rows, lanes] * inverse).astype(jnp.int32).astype(jnp.int16)
                out_q[slot, pl.ds(pl.multiple_of(p * QUARTER + r * 32, 32), 32), :] = v
            return carry

        lax.fori_loop(0, QUARTER // 32, body, 0)
        message_of(key).start()

    def arrived(*keys):
        for key in keys:
            message_of(key).wait_recv()

    def corner_copy(dx, dy):
        k = dx * 4 + dy
        return pltpu.make_async_remote_copy(
            src_ref=corner_out.at[k], dst_ref=corner_in.at[k], send_sem=c_send.at[k],
            recv_sem=c_recv.at[k], device_id=peer(dx, dy), device_id_type=MESH,
        )

    def code_of(peak):
        return jnp.ceil(jnp.log(jnp.maximum(peak, 1e-30)) * CODE) + 1.0

    corner_swap.wait()
    for dx, dy in ORDER[:-1]:
        i = chunk(dx, dy)
        both = corners[core, i] + corners2[i]
        code = code_of(jnp.max(jnp.abs(both), axis=0, keepdims=True))
        code = jnp.broadcast_to(code, (16, 128)).astype(jnp.int32).astype(jnp.int16)
        corner_out[dx * 4 + dy, pl.ds(128, 16), :] = code
        both = jnp.round(both * (1.0 / scale_of(code)[0:1]))
        corner_out[dx * 4 + dy, pl.ds(0, 128), :] = both.astype(jnp.int32).astype(jnp.int16)
        corner_copy(dx, dy).start()
    weight_swap.wait()

    def gradient_of(dx, dy):
        i = chunk(dx, dy)
        act_copy(dx, dy).wait()

        def product(n, carry):
            lanes = pl.ds(pl.multiple_of(n * 256, 256), 256)
            own = pl.ds(pl.multiple_of((i * 2 + core) * ROWS + n * 256, 256), 256)
            g[i, :, lanes] = dot(weights[:, pl.ds(0, TOK)], act[:, own], None) + dot(
                weights[:, pl.ds(TOK, TOK)], act2[i, :, lanes], None
            )
            return carry

        lax.fori_loop(0, ROWS // 256, product, 0)
        ring = "b1" if dx else "b0"
        sends = {2: [((ring, "p1lo"), 2), ((ring, "p1hi"), 3)], 1: [((ring, "p2hi"), 3)], 3: [((ring, "p2lo"), 2)], 0: []}[dy]
        for key, q in sends:
            send(key, i, q, peak_of(i, q))

    def across(dy):
        for q in (0, 1):
            send(("x1", dy, q), chunk(1, dy), q, peak_of(chunk(1, dy), q))

    def collect(table):
        for b in range(8):
            rows = pl.ds(b * 32, 32)
            total = jnp.zeros((32, 128), jnp.float32)
            for c in range(16):
                total = total + jnp.where(column[rows, :] == c, table[b * 16 + c][None, :], 0.0)
            spread_values[rows, :] = total * here[rows, :]
        return dot_last(pick, spread_values[...])

    def scatter(values):
        spread = lax.dot_general(
            values, pick, (((0,), (0,)), ((), ())), precision=HIGHEST, preferred_element_type=jnp.float32
        )
        spread_values[...] = spread * here[...]
        wanted = lax.broadcasted_iota(jnp.int32, (16, 32, 128), 0)
        for b in range(8):
            rows = pl.ds(b * 32, 32)
            hit = jnp.where(column[rows, :][None] == wanted, spread_values[rows, :][None], 0.0)
            coefs[pl.ds(b * 16, 16), :] = jnp.sum(hit, axis=1)

    def inverse():
        return dot(dot_last(ftm[...], coefs[...]), fm[...])

    def sent_copy(k):
        return pltpu.make_async_remote_copy(
            src_ref=sent, dst_ref=sent_in.at[k], send_sem=r_send.at[k],
            recv_sem=r_recv.at[k], device_id=rep_peer(k), device_id_type=MESH,
        )

    def chunk_rows(dx, dy, first=0, count=ROWS):
        return pl.ds(pl.multiple_of(shard(dx, dy) * ROWS + first, 16), count)

    copies = {}

    def gather(key, rows, target):
        k = GATHER[key]
        copies[key] = pltpu.make_async_remote_copy(
            src_ref=new_w.at[rows], dst_ref=new_w.at[rows], send_sem=w_send.at[k],
            recv_sem=w_recv.at[k], device_id=target, device_id_type=MESH,
        )
        copies[key].start()

    lower = lax.rem(z, 2)
    mine, theirs = lower * (2 * PART + KEPT), (1 - lower) * (2 * PART + KEPT)

    def rows_of_part(dx, dy, p):
        if p == 2:
            return chunk_rows(dx, dy, 2 * PART, KEPT)
        return chunk_rows(dx, dy, mine + p * PART, PART)

    def share(dx, dy, p):
        rows = rows_of_part(dx, dy, p)
        if dx == 0:
            gather(("x", dy, p), rows, x_peer if p == 2 else x_hi_peer)
        if (dx, dy) != (0, 0):
            if p < 2:
                gather(("z-" if p else "z+", dx, dy), rows, behind if p else ahead)
            gather(("core", dx, dy, p), rows, sibling)

    def landed(*keys):
        for key in keys:
            copies[key].wait_recv()

    def got_x(dy):
        for p in (0, 1):
            landed(("x", dy, p))
            share(1, dy, p)

    def got_x_kept(dy):
        landed(("x", dy, 2))
        share(1, dy, 2)

    def got_z(dx, dy):
        landed(("z+", dx, dy), ("z-", dx, dy))
        gather(("corez", dx, dy), chunk_rows(dx, dy, theirs, 2 * PART), sibling)

    def first_y():
        landed(("y+", 0))
        gather(("y++", 0), rows_of_part(0, 3, 0), up)
        share(0, 3, 0)
        landed(("y-", 1))
        gather(("y--", 0), rows_of_part(0, 1, 1), down)
        share(0, 1, 1)

    def second_y():
        landed(("y+", 1))
        share(0, 3, 1)
        landed(("y-", 0))
        share(0, 1, 0)

    def third_y():
        landed(("y++", 0))
        share(0, 2, 0)
        landed(("y--", 0))
        share(0, 2, 1)

    def first_kept():
        landed(("y+", 2))
        gather(("y++", 1), chunk_rows(0, 3, 2 * PART, KEPT // 2), up)
        share(0, 3, 2)
        landed(("y-", 2))
        gather(("y--", 1), chunk_rows(0, 1, 2 * PART + KEPT // 2, KEPT // 2), down)
        share(0, 1, 2)

    def second_kept():
        landed(("y++", 1), ("y--", 1))
        share(0, 2, 2)

    def forward(ring, leg, dx, dy, q, *keys):
        arrived(*keys)
        send((ring, leg), chunk(dx, dy), q, add_received(chunk(dx, dy), q, keys))

    def b_second(ring, dx):
        forward(ring, "p3lo", dx, 1, 2, (ring, "p1lo"))
        forward(ring, "p3hi", dx, 3, 3, (ring, "p1hi"))

    def a_first():
        forward("a0", "p1lo", 0, 2, 0, ("x1", 2, 0))
        forward("a0", "p1hi", 0, 2, 1, ("x1", 2, 1))

    def a_direct():
        forward("a0", "p2hi", 0, 1, 1, ("x1", 1, 1))
        forward("a0", "p2lo", 0, 3, 0, ("x1", 3, 0))

    def a_second():
        forward("a0", "p3lo", 0, 1, 0, ("x1", 1, 0), ("a0", "p1lo"))
        forward("a0", "p3hi", 0, 3, 1, ("x1", 3, 1), ("a0", "p1hi"))

    def b_last():
        for q, half in ((2, "lo"), (3, "hi")):
            keys = [("b1", "p2" + half), ("b1", "p3" + half)]
            arrived(*keys)
            send(("x3", q), chunk(1, 0), q, add_received(chunk(1, 0), q, keys))

    lane = lax.broadcasted_iota(jnp.int32, (8, 128), 1)
    pick = jnp.where(lane // 16 == lax.broadcasted_iota(jnp.int32, (8, 128), 0), 1.0, 0.0)

    def prepare():
        for copy in second:
            copy.wait()
        row = lax.rem(lax.broadcasted_iota(jnp.int32, (32, 128), 1), 16)
        for b in range(8):
            places = lax.dot_general(
                band[:, b, :].astype(jnp.float32), pick, (((0,), (0,)), ((), ())),
                precision=HIGHEST, preferred_element_type=jnp.float32,
            )
            places = jnp.round(places).astype(jnp.int32)
            rows = pl.ds(b * 32, 32)
            column[rows, :] = jnp.bitwise_and(places, 63)
            here[rows, :] = jnp.where(jnp.right_shift(places, 6) == row, 1.0, 0.0)
        low_sum[...] = dot_last(fm[...], dot(fm[...], mom[...])) * beta_decay

    def band_of_replica():
        i = chunk(0, 0)
        total = low_sum[...] + (corners[core, i] + corners2[i])
        for dx, dy in ORDER[:-1]:
            k = dx * 4 + dy
            corner_copy(dx, dy).wait()
            values = corner_in[k, pl.ds(0, 128), :].astype(jnp.int32).astype(jnp.float32)
            total = total + values * scale_of(corner_in[k, pl.ds(128, 16), :])[0:1]
        sent[...] = collect(total)
        for k in range(1, N_REP):
            sent_copy(k).start()

    def new_rows():
        sent_in[0] = sent[...]
        for k in range(1, N_REP):
            sent_copy(k).wait()
        mean = sent_in[rep]
        for r in range(1, N_REP):
            mean = mean + sent_in[lax.rem(N_REP + rep - r, N_REP)]
        scatter(mean * (1.0 / N_REP))
        def update(first, count):
            local_rows = pl.ds(pl.multiple_of(first, 16), count)
            change = dot(dot_last(ftm[local_rows, :], coefs[...]), fm[...])
            new_w[chunk_rows(0, 0, first, count), :] = (par[local_rows, :] - step_size * change).astype(jnp.bfloat16)

        update(mine, PART)
        gather(("y+", 0), rows_of_part(0, 0, 0), up)
        share(0, 0, 0)
        update(mine + PART, PART)
        gather(("y-", 1), rows_of_part(0, 0, 1), down)
        gather(("y+", 1), rows_of_part(0, 0, 1), up)
        gather(("y-", 0), rows_of_part(0, 0, 0), down)
        share(0, 0, 1)

    def kept_rows():
        def update(first, count):
            local_rows = pl.ds(pl.multiple_of(first, 16), count)
            change = dot(dot_last(ftm[local_rows, :], coefs[...]), fm[...])
            new_w[chunk_rows(0, 0, first, count), :] = (par[local_rows, :] - step_size * change).astype(jnp.bfloat16)

        update(2 * PART, KEPT)
        gather(("y+", 2), rows_of_part(0, 0, 2), up)
        gather(("y-", 2), rows_of_part(0, 0, 2), down)
        share(0, 0, 2)
        update(theirs, 2 * PART)
        gather(("core", 0, 0, 0), chunk_rows(0, 0), sibling)

    def remainder():
        scatter(sent[...])
        base[...] = beta_decay * mom[...] - inverse()

    def finish(q, keys):
        arrived(*keys)
        add_received(chunk(0, 0), q, keys)
        lanes = pl.ds(q * QUARTER, QUARTER)
        new_m[0, :, lanes] = base[:, lanes] + g[chunk(0, 0), lanes, :].T

    def finish_a():
        finish(0, [("x1", 0, 0), ("a0", "p2lo"), ("a0", "p3lo")])
        finish(1, [("x1", 0, 1), ("a0", "p2hi"), ("a0", "p3hi")])

    def finish_b():
        finish(2, [("b0", "p2lo"), ("b0", "p3lo"), ("x3", 2)])
        finish(3, [("b0", "p2hi"), ("b0", "p3hi"), ("x3", 3)])

    gradient_of(*ORDER[0])
    across(2)
    gradient_of(*ORDER[1])
    prepare()
    gradient_of(*ORDER[2])
    gradient_of(*ORDER[3])
    band_of_replica()
    across(1)
    across(3)
    b_second('b1',1)
    gradient_of(*ORDER[4])
    gradient_of(*ORDER[5])
    new_rows()
    kept_rows()
    gradient_of(*ORDER[6])
    a_first()
    first_y()
    second_y()
    across(0)
    b_second('b0',0)
    got_x(0)
    third_y()
    a_direct()
    b_last()
    got_x(3)
    got_x(1)
    first_kept()
    a_second()
    got_x(2)
    second_kept()
    remainder()
    got_z(0,3)
    got_z(0,1)
    got_x_kept(0)
    gradient_of(*ORDER[7])
    finish_b()
    got_z(0,2)
    got_z(1,0)
    finish_a()
    got_x_kept(3)
    got_x_kept(1)
    got_x_kept(2)
    got_z(1,3)
    got_z(1,1)
    got_z(1,2)

    for key, copy in copies.items():
        copy.wait_send()
        if key[0] in ("core", "corez"):
            copy.wait_recv()
    for key in MESSAGES:
        message_of(key).wait_send()


def local(activations, cotangent, momentum, params, band, f, ft):
    any_space = pl.BlockSpec(memory_space=pl.ANY)
    i16, f32, bf16 = jnp.int16, jnp.float32, jnp.bfloat16
    dma = pltpu.SemaphoreType.DMA
    n = len(MESSAGES)
    return pl.pallas_call(
        kernel,
        out_shape=(
            pltpu.VMEM((16 * ROWS, COLS), bf16),
            pltpu.VMEM((1, ROWS, COLS), f32),
        ),
        in_specs=[any_space] * 7,
        out_specs=(pl.BlockSpec(memory_space=pltpu.VMEM), pl.BlockSpec(memory_space=pltpu.VMEM)),
        scratch_shapes=[
            pltpu.VMEM((TOK, 16 * ROWS), bf16),
            pltpu.VMEM((8, TOK, ROWS), bf16),
            pltpu.VMEM((TOK, COLS), bf16),
            pltpu.VMEM((ROWS, COLS), f32),
            pltpu.VMEM((ROWS, COLS), f32),
            pltpu.VMEM((8, 8, 32), jnp.int32),
            pltpu.VMEM((128, 512), f32),
            pltpu.VMEM((512, 128), f32),
            pltpu.VMEM((256, TOK), bf16),
            pltpu.VMEM((512, 256), bf16),
            pltpu.VMEM((COLS, 2 * TOK), bf16),
            pltpu.VMEM((8, COLS, ROWS), f32),
            pltpu.VMEM((ROWS, COLS), f32),
            pltpu.VMEM((256, 128), jnp.int32),
            pltpu.VMEM((256, 128), f32),
            pltpu.VMEM((n, PACKED, 128), i16),
            pltpu.VMEM((n, PACKED, 128), i16),
            pltpu.VMEM((2, 8, 128, 128), f32),
            pltpu.VMEM((8, 128, 128), f32),
            pltpu.VMEM((8, 144, 128), i16),
            pltpu.VMEM((8, 144, 128), i16),
            pltpu.VMEM((8, 256), f32),
            pltpu.VMEM((N_REP, 8, 256), f32),
            pltpu.VMEM((256, 128), f32),
            pltpu.VMEM((128, 128), f32),
            pltpu.VMEM((128, 128), f32),
            dma((6,)), dma((8,)), dma((8,)), dma((8,)), dma((2,)), dma((2,)), dma((n,)), dma((n,)), dma((8,)), dma((8,)),
            dma((N_REP,)), dma((N_REP,)), dma((len(GATHERS),)), dma((len(GATHERS),)),
        ],
        compiler_params=pltpu.CompilerParams(
            collective_id=0, has_side_effects=True, vmem_limit_bytes=48 * 2**20
        ),
    )(activations, cotangent, momentum, params, band, f, ft)


def step(activations, cotangent, momentum, params, band):
    f = band_matrix()
    return local(activations, cotangent, momentum, params, band, jnp.asarray(f), jnp.asarray(f.T.copy()))


def solution(mesh):
    return jax.shard_map(
        step,
        mesh=mesh,
        in_specs=(
            P(("rep", "fsdp"), None),
            P(("rep", "fsdp"), None),
            P("rep", "fsdp", None),
            P("fsdp", None),
            P("fsdp", None, None),
        ),
        out_specs=(P(), P("rep", "fsdp", None)),
        check_vma=False,
    )
```

time: 101 us -> 72 us (0.71)
  Pallas kernels: 96.2 us -> 66.9 us
    pallas_call x1, Pallas kernels: 96.2 us -> 66.9 us  [local(): pl.pallas_call(kernel, out_shape=(pltpu.VMEM((16 * ROWS, COLS), bf16), pl...]
where the time goes in v2:
time: 72 us; the launch traced here: 71.9 us
  Pallas kernels  66.9 us (93%)
  local copies, waits for them, and re-layouts  4.37 us (6%)
    pallas_call x1, Pallas kernels, local(): pl.pallas_call(kernel, out_shape=(pltpu.VMEM((16 * ROWS, COLS), bf16), pl...  66.9 us
    unnamed x2, local copies, waits for them, and re-layouts  4.37 us

profile of v2, /device:TPU:1, one launch (start us, length us, event | category | flops | bytes accessed | tf_op | source)
XLA Modules:
  0.0 71.9 jit_solution(14471565191861184151)
XLA Ops:
  0.6 66.9 %shard_map.86 = (bf16[8192,512]{1,0:T(8,128)(2,1)S(1)}, f32[1,512,512]{2,1,0:T(8,128)S(1)}) custom-call(bf16[384,8192]{1,0:T(8,128)(2,1)} %act_hbm.1, bf16[384,512]{1,0:T(8,128)(2,1)} %cot_hbm.1, f32[1,512,512]{2,1,0:T(8,128)} %mom_hbm.1, f32[512,512]{1,0:T(8,128)} %par_hbm.1, s32[8,8,32]{2,1,0:T(8,128)} %band_hbm.1, f32[128,512]{1,0:T(8,128)} %constant.4.clone.f_hbm, ...), custom_call_target="tpu_custom_call" | custom-call | tf_op jit(solution)/shard_map/pallas_call | solution.py:557
  67.6 3.4 %copy.11 = bf16[8192,512]{1,0:T(8,128)(2,1)} copy(bf16[8192,512]{1,0:T(8,128)(2,1)S(1)} %get-tuple-element.2) | data formatting | bytes 16777216
  71.0 1.0 %copy.12 = f32[1,512,512]{2,1,0:T(8,128)} copy(f32[1,512,512]{2,1,0:T(8,128)S(1)} %get-tuple-element.3) | data formatting | bytes 2097152

commit v3 on v2

--- a/solution.py
+++ b/solution.py
@@ -57,7 +57,7 @@
 SLOT = {key: i for i, key in enumerate(MESSAGES)}
 OTHERS = [(dx, dy) for dx in (0, 1) for dy in range(4) if (dx, dy) != (0, 0)]
 GATHERS = (
-    [("core", dx, dy, p) for dx in (0, 1) for dy in range(4) for p in (0, 1, 2)]
+    [("core", dx, dy) for dx in (0, 1) for dy in range(4)]
     + [("corez", dx, dy) for dx, dy in OTHERS]
     + [(way, p) for way in ("y+", "y-") for p in (0, 1, 2)]
     + [(way, p) for way in ("y++", "y--") for p in (0, 1)]
@@ -96,26 +96,26 @@
     ahead = (x_hi * 8 + lax.rem(z + 1, 8), fsdp)
     behind = (x_hi * 8 + lax.rem(z + 7, 8), fsdp)
 
+    def load(src, dst, i):
+        copy = pltpu.make_async_copy(src, dst, local_sem.at[i])
+        copy.start()
+        return copy
+
+    first = [load(cot_hbm, cot, 0), load(f_hbm, fm, 1), load(ft_hbm, ftm, 4)]
+
+    def act_local(i):
+        lanes = pl.ds(pl.multiple_of(i * 2 * ROWS, 2 * ROWS), 2 * ROWS)
+        return pltpu.make_async_copy(act_hbm.at[:, lanes], act.at[:, lanes], act_sem.at[i])
+
+    for i in range(8):
+        act_local(i).start()
+    second = [load(band_hbm, band, 2), load(mom_hbm.at[0], mom, 3), load(par_hbm, par, 5)]
+
     barrier = pltpu.get_barrier_semaphore()
     greeted = [rep_peer(k) for k in range(1, N_REP)] + [x_hi_peer, sibling]
     greeted += [peer(dx, dy) for dx, dy in ORDER[:-1]]
     for other in greeted:
         pl.semaphore_signal(barrier, inc=1, device_id=other, device_id_type=MESH)
-
-    def load(src, dst, i):
-        copy = pltpu.make_async_copy(src, dst, local_sem.at[i])
-        copy.start()
-        return copy
-
-    first = [load(cot_hbm, cot, 0), load(f_hbm, fm, 1), load(ft_hbm, ftm, 4)]
-
-    def act_local(i):
-        lanes = pl.ds(pl.multiple_of(i * 2 * ROWS, 2 * ROWS), 2 * ROWS)
-        return pltpu.make_async_copy(act_hbm.at[:, lanes], act.at[:, lanes], act_sem.at[i])
-
-    for i in range(8):
-        act_local(i).start()
-    second = [load(band_hbm, band, 2), load(mom_hbm.at[0], mom, 3), load(par_hbm, par, 5)]
 
     for copy in first:
         copy.wait()
@@ -244,17 +244,18 @@
     def code_of(peak):
         return jnp.ceil(jnp.log(jnp.maximum(peak, 1e-30)) * CODE) + 1.0
 
-    corner_swap.wait()
-    for dx, dy in ORDER[:-1]:
-        i = chunk(dx, dy)
-        both = corners[core, i] + corners2[i]
-        code = code_of(jnp.max(jnp.abs(both), axis=0, keepdims=True))
-        code = jnp.broadcast_to(code, (16, 128)).astype(jnp.int32).astype(jnp.int16)
-        corner_out[dx * 4 + dy, pl.ds(128, 16), :] = code
-        both = jnp.round(both * (1.0 / scale_of(code)[0:1]))
-        corner_out[dx * 4 + dy, pl.ds(0, 128), :] = both.astype(jnp.int32).astype(jnp.int16)
-        corner_copy(dx, dy).start()
-    weight_swap.wait()
+    def corners_out():
+        corner_swap.wait()
+        for dx, dy in ORDER[:-1]:
+            i = chunk(dx, dy)
+            both = corners[core, i] + corners2[i]
+            code = code_of(jnp.max(jnp.abs(both), axis=0, keepdims=True))
+            code = jnp.broadcast_to(code, (16, 128)).astype(jnp.int32).astype(jnp.int16)
+            corner_out[dx * 4 + dy, pl.ds(128, 16), :] = code
+            both = jnp.round(both * (1.0 / scale_of(code)[0:1]))
+            corner_out[dx * 4 + dy, pl.ds(0, 128), :] = both.astype(jnp.int32).astype(jnp.int16)
+            corner_copy(dx, dy).start()
+        weight_swap.wait()
 
     def gradient_of(dx, dy):
         i = chunk(dx, dy)
@@ -335,7 +336,6 @@
         if (dx, dy) != (0, 0):
             if p < 2:
                 gather(("z-" if p else "z+", dx, dy), rows, behind if p else ahead)
-            gather(("core", dx, dy, p), rows, sibling)
 
     def landed(*keys):
         for key in keys:
@@ -346,9 +346,12 @@
             landed(("x", dy, p))
             share(1, dy, p)
 
+    def to_core(dx, dy):
+        gather(("core", dx, dy), chunk_rows(dx, dy, lower * (2 * PART), 2 * PART + KEPT), sibling)
+
     def got_x_kept(dy):
         landed(("x", dy, 2))
-        share(1, dy, 2)
+        to_core(1, dy)
 
     def got_z(dx, dy):
         landed(("z+", dx, dy), ("z-", dx, dy))
@@ -378,13 +381,16 @@
         landed(("y+", 2))
         gather(("y++", 1), chunk_rows(0, 3, 2 * PART, KEPT // 2), up)
         share(0, 3, 2)
+        to_core(0, 3)
         landed(("y-", 2))
         gather(("y--", 1), chunk_rows(0, 1, 2 * PART + KEPT // 2, KEPT // 2), down)
         share(0, 1, 2)
+        to_core(0, 1)
 
     def second_kept():
         landed(("y++", 1), ("y--", 1))
         share(0, 2, 2)
+        to_core(0, 2)
 
     def forward(ring, leg, dx, dy, q, *keys):
         arrived(*keys)
@@ -439,7 +445,7 @@
             values = corner_in[k, pl.ds(0, 128), :].astype(jnp.int32).astype(jnp.float32)
             total = total + values * scale_of(corner_in[k, pl.ds(128, 16), :])[0:1]
         sent[...] = collect(total)
-        for k in range(1, N_REP):
+        for k in (12, 4, 11, 13, 3, 5, 10, 14, 2, 6, 9, 15, 1, 7, 8):
             sent_copy(k).start()
 
     def new_rows():
@@ -475,7 +481,7 @@
         gather(("y-", 2), rows_of_part(0, 0, 2), down)
         share(0, 0, 2)
         update(theirs, 2 * PART)
-        gather(("core", 0, 0, 0), chunk_rows(0, 0), sibling)
+        gather(("core", 0, 0), chunk_rows(0, 0), sibling)
 
     def remainder():
         scatter(sent[...])
@@ -495,13 +501,14 @@
         finish(2, [("b0", "p2lo"), ("b0", "p3lo"), ("x3", 2)])
         finish(3, [("b0", "p2hi"), ("b0", "p3hi"), ("x3", 3)])
 
+    prepare()
+    corners_out()
     gradient_of(*ORDER[0])
-    across(2)
     gradient_of(*ORDER[1])
-    prepare()
     gradient_of(*ORDER[2])
     gradient_of(*ORDER[3])
     band_of_replica()
+    across(2)
     across(1)
     across(3)
     b_second('b1',1)
@@ -509,27 +516,27 @@
     gradient_of(*ORDER[5])
     new_rows()
     kept_rows()
+    a_first()
     gradient_of(*ORDER[6])
-    a_first()
+    gradient_of(*ORDER[7])
     first_y()
     second_y()
     across(0)
+    got_x(0)
     b_second('b0',0)
-    got_x(0)
     third_y()
     a_direct()
-    b_last()
     got_x(3)
     got_x(1)
+    b_last()
     first_kept()
     a_second()
     got_x(2)
     second_kept()
     remainder()
+    got_x_kept(0)
     got_z(0,3)
     got_z(0,1)
-    got_x_kept(0)
-    gradient_of(*ORDER[7])
     finish_b()
     got_z(0,2)
     got_z(1,0)

time: 72 us -> 71 us (0.986)
  Pallas kernels: 66.9 us -> 65.9 us
    pallas_call x1, Pallas kernels: 66.9 us -> 65.9 us  [local(): pl.pallas_call(kernel, out_shape=(pltpu.VMEM((16 * ROWS, COLS), bf16), pl...]
where the time goes in v3:
time: 71 us; the launch traced here: 70.9 us
  Pallas kernels  65.9 us (93%)
  local copies, waits for them, and re-layouts  4.37 us (6%)
    pallas_call x1, Pallas kernels, local(): pl.pallas_call(kernel, out_shape=(pltpu.VMEM((16 * ROWS, COLS), bf16), pl...  65.9 us
    unnamed x2, local copies, waits for them, and re-layouts  4.37 us

profile of v3, /device:TPU:1, one launch (start us, length us, event | category | flops | bytes accessed | tf_op | source)
XLA Modules:
  0.0 70.9 jit_solution(7965643548854540595)
XLA Ops:
  0.6 65.9 %shard_map.86 = (bf16[8192,512]{1,0:T(8,128)(2,1)S(1)}, f32[1,512,512]{2,1,0:T(8,128)S(1)}) custom-call(bf16[384,8192]{1,0:T(8,128)(2,1)} %act_hbm.1, bf16[384,512]{1,0:T(8,128)(2,1)} %cot_hbm.1, f32[1,512,512]{2,1,0:T(8,128)} %mom_hbm.1, f32[512,512]{1,0:T(8,128)} %par_hbm.1, s32[8,8,32]{2,1,0:T(8,128)} %band_hbm.1, f32[128,512]{1,0:T(8,128)} %constant.4.clone.f_hbm, ...), custom_call_target="tpu_custom_call" | custom-call | tf_op jit(solution)/shard_map/pallas_call | solution.py:564
  66.5 3.4 %copy.11 = bf16[8192,512]{1,0:T(8,128)(2,1)} copy(bf16[8192,512]{1,0:T(8,128)(2,1)S(1)} %get-tuple-element.2) | data formatting | bytes 16777216
  69.9 1.0 %copy.12 = f32[1,512,512]{2,1,0:T(8,128)} copy(f32[1,512,512]{2,1,0:T(8,128)S(1)} %get-tuple-element.3) | data formatting | bytes 2097152
